TPU v7x, 32 devices: a whole 2x2x4 slice. The times are simulated.
32 devices in a mesh: sy: 4 (over y, x), sz: 8 (over z, core).
Axes of the slice: x: 2, y: 2, z: 4, core: 2. Of those that a mesh axis runs over, the one named last changes fastest.
Arguments:
- labels: int32 [16, 256, 256], P(None, 'sy', 'sz'), may hold values from 0 to 3
- wall_dist: bfloat16 [16, 256, 256], P(None, 'sy', 'sz'), may hold values from -5 to 5
- material_table: bfloat16 [4, 16], replicated, may hold values from -4 to 4
- dist_weight: bfloat16 [16], replicated, may hold values from -4 to 4
- conv_weight: bfloat16 [27, 16, 16], replicated, may hold values from -0.3125 to 0.3125
- down_weight: bfloat16 [8, 64, 16], replicated, may hold values from -0.5 to 0.5
- mix_weight: bfloat16 [64, 128, 128], P('sz'), may hold values from -0.5 to 0.5
- cotangent: bfloat16 [64, 8, 128, 128], P('sz', None, 'sy'), may hold values from -6 to 6
Outputs:
- mid_features: bfloat16 [64, 8, 128, 128], P('sz', None, 'sy')
- mix_grad: float32 [64, 128, 128], P('sz', 'sy')
- down_grad: float32 [8, 64, 16], replicated
- conv_grad: float32 [27, 16, 16], replicated
All inputs are finite; a program needn't handle non-finite values.
Results may differ from a plain program's by a relative error of at most 0.0084.
Values may be sent and summed in bfloat16 or wider, within the bound.
A program may use at most 192 MiB of HBM per device.

v0:
```python
import math

import jax
import jax.numpy as jnp
import numpy as np
from jax import lax
from jax.sharding import PartitionSpec as P


def extended(value, sides, width):
    for axis, dim in sides:
        size, length = (lax.axis_size(axis), value.shape[dim])
        up = [(i, (i + 1) % size) for i in range(size - 1)]
        down = [(j, i) for i, j in up]
        last = lax.slice_in_dim(value, length - width, length, axis=dim)
        first = lax.slice_in_dim(value, 0, width, axis=dim)
        before = lax.ppermute(last, axis, up)
        after = lax.ppermute(first, axis, down)
        value = jnp.concatenate([before, value, after], axis=dim)
    return value


def silu_slope(values):
    sigma = jax.nn.sigmoid(values)
    return sigma * (1.0 + values * (1.0 - sigma))


def window_picks(half):
    picks = np.zeros((2 * half + 2, 4 * half), np.float32)
    for u in range(4):
        for h in range(half):
            picks[2 * h + u, u * half + h] = 1.0
    return jnp.asarray(picks, jnp.bfloat16)


def dot(spec, left, right):
    return jnp.einsum(spec, left, right, preferred_element_type=jnp.float32)


def per_device(
    labels, wall_dist, material_table, dist_weight, conv_weight, down_weight, mix_weight, cotangent
):
    depth, rows_y, rows_z = labels.shape
    materials, channels = material_table.shape
    wide_channels = down_weight.shape[1]
    count_y = lax.axis_size("sy")
    count_z = lax.axis_size("sz")
    half_x, half_y, half_z = depth // 2, rows_y // 2, rows_z // 2
    plane = half_x * half_y
    cells = half_z * plane
    corners = [(a, b, c) for a in range(2) for b in range(2) for c in range(2)]

    taps = jnp.transpose(conv_weight, (0, 2, 1)).reshape(3, 3, 3, channels, channels)
    conv_matrix = jnp.concatenate(
        [jnp.pad(taps, ((a, 1 - a), (b, 1 - b), (c, 1 - c), (0, 0), (0, 0))) for a, b, c in corners],
        axis=4,
    ).reshape(64 * channels, 8 * channels)
    down_matrix = jnp.concatenate([down_weight[t] for t in range(8)], axis=1)

    stacked = jnp.stack([(labels + 1).astype(jnp.bfloat16), wall_dist])
    widened = extended(stacked, (("sy", 2), ("sz", 3)), 1)
    windows = dot("txyz,yq->txzq", widened, window_picks(half_y)).astype(jnp.bfloat16)
    windows = dot("txzq,zr->txrq", windows, window_picks(half_z)).astype(jnp.bfloat16)
    windows = jnp.pad(windows, ((0, 0), (1, 1), (0, 0), (0, 0)))
    windows = windows.reshape(2, half_x + 1, 2, 4, half_z, 4, half_y)
    windows = jnp.stack(
        [windows[:, w // 2 : w // 2 + half_x, w % 2] for w in range(4)], axis=1
    )
    windows = jnp.transpose(windows, (0, 1, 5, 3, 4, 2, 6)).reshape(2, 64, cells)
    features = [(windows[0] == entry + 1).astype(jnp.bfloat16) for entry in range(materials)]
    features = jnp.concatenate(features + [windows[1]], axis=0)
    own = jnp.arange(64)[:, None] == (jnp.arange(64 * channels) // channels)[None, :]
    table = jnp.concatenate([material_table, dist_weight[None]], axis=0)
    table = jnp.tile(table, (1, 64))
    table = jnp.concatenate(
        [jnp.where(own, table[f][None], jnp.zeros((), table.dtype)) for f in range(materials + 1)],
        axis=0,
    )
    patches = dot("fm,fn->mn", table, features).astype(jnp.bfloat16)

    pre_act = dot("km,kn->mn", conv_matrix, patches)
    hidden = jax.nn.silu(pre_act).astype(jnp.bfloat16)
    coarse = dot("om,mn->on", down_matrix, hidden).astype(jnp.bfloat16)
    coarse = coarse.reshape(wide_channels, half_z, plane)
    channel_coarse = lax.all_to_all(coarse, "sz", split_axis=0, concat_axis=1, tiled=True)
    mixed_pre = dot("czw,cwp->cpz", mix_weight, channel_coarse)
    mid_features = jax.nn.silu(mixed_pre).astype(jnp.bfloat16).reshape(cotangent.shape)
    gradient = cotangent.astype(jnp.float32).reshape(mixed_pre.shape)
    mixed_grad = (gradient * silu_slope(mixed_pre)).astype(jnp.bfloat16)
    channel_grad = dot("czw,cpz->cwp", mix_weight, mixed_grad).astype(jnp.bfloat16)
    coarse_grad = lax.all_to_all(channel_grad, "sz", split_axis=1, concat_axis=0, tiled=True)
    coarse_grad = coarse_grad.reshape(wide_channels, cells)
    mix_partial = dot("cpz,cwp->czw", mixed_grad, channel_coarse)
    mix_grad = lax.psum_scatter(mix_partial, "sy", scatter_dimension=1, tiled=True) / math.sqrt(
        plane * count_y
    )

    down_partial = dot("on,mn->om", coarse_grad, hidden)
    hidden_grad = dot("om,on->mn", down_matrix, coarse_grad)
    pre_grad = (hidden_grad * silu_slope(pre_act)).astype(jnp.bfloat16)
    correlated = dot("kn,mn->km", patches, pre_grad).reshape(4, 4, 4, channels, 8 * channels)
    conv_partial = sum(
        correlated[a : a + 3, b : b + 3, c : c + 3, :, t * channels : (t + 1) * channels]
        for t, (a, b, c) in enumerate(corners)
    )
    width = 8 * channels
    parts = jnp.concatenate([down_partial, conv_partial.reshape(-1, width)], axis=0)
    parts = lax.psum(parts, ("sy", "sz"))
    cells_fine = depth * rows_y * count_y * rows_z * count_z
    cells_coarse = cells_fine // 8
    down_total = parts[:wide_channels].reshape(wide_channels, 8, channels)
    conv_total = parts[wide_channels:].reshape(27, channels, channels)
    down_grad = jnp.transpose(down_total, (1, 0, 2)) / math.sqrt(cells_coarse)
    conv_grad = jnp.transpose(conv_total, (0, 2, 1)) / math.sqrt(cells_fine)
    return (mid_features, mix_grad, down_grad, conv_grad)


def solution(mesh):
    in_specs = (
        P(None, "sy", "sz"),
        P(None, "sy", "sz"),
        P(),
        P(),
        P(),
        P(),
        P("sz", None, None),
        P("sz", None, "sy", None),
    )
    out_specs = (P("sz", None, "sy", None), P("sz", "sy", None), P(), P())
    return jax.shard_map(
        per_device, mesh=mesh, in_specs=in_specs, out_specs=out_specs, check_vma=False
    )
```

profile of v0, /device:TPU:0, one launch (start us, length us, event | category | flops | bytes accessed | tf_op | source)
XLA Modules:
  0.0 178.1 jit_solution(4954479846756233423)
XLA Ops:
  7.2 1.0 fusion.37
  8.2 1.1 slice_maximum_fusion
  9.4 4.9 %collective-permute-start = (bf16[2,16,1,32]{2,3,1,0:T(8,128)(2,1)S(1)}, bf16[2,16,1,32]{2,3,1,0:T(8,128)(2,1)S(1)}, u32[]{:S(2)}, u32[]{:S(2)}) collective-permute-start(bf16[2,16,1,32]{2,3,1,0:T(8,128)(2,1)S(1)} %get-tuple-element.28), channel_id=1, source_target_pairs={{0,8},{8,16},{16,24},{1,9},{9,17},{17,25},{2,10},{10,18},{18,26},{... | collective-permute-start | bytes 6152 | tf_op jit(solution)/shard_map/ppermute | solution.py:17
  14.2 1.3 collective-permute-start.1
  15.6 0.8 slice_bitcast_fusion
  16.8 0.7 tile.33
  17.5 0.7 constant_dynamic-update-slice_fusion.7
  18.2 0.7 constant_dynamic-update-slice_fusion.6
  18.9 0.7 constant_dynamic-update-slice_fusion.5
  19.6 0.7 constant_dynamic-update-slice_fusion.4
  20.3 0.7 constant_dynamic-update-slice_fusion.3
  21.0 0.7 constant_dynamic-update-slice_fusion.2
  21.7 0.7 constant_dynamic-update-slice_fusion.1
  22.6 0.7 constant_dynamic-update-slice_fusion
  23.3 1.0 copy.45
  24.3 3.0 %collective-permute-done.1 = bf16[2,16,1,32]{2,3,1,0:T(8,128)(2,1)S(1)} collective-permute-done((bf16[2,16,1,32]{2,3,1,0:T(8,128)(2,1)S(1)}, bf16[2,16,1,32]{2,3,1,0:T(8,128)(2,1)S(1)}, u32[]{:S(2)}, u32[]{:S(2)}) %collective-permute-start.1) | collective-permute-done | bytes 2080 | tf_op jit(solution)/shard_map/ppermute | solution.py:18
  27.5 1.3 collective-permute-start.2
  28.8 1.3 collective-permute-start.3
  30.6 3.9 %concatenate.23 = bf16[4,4,4,16,128]{4,3,2,1,0:T(8,128)(2,1)} concatenate(bf16[4,4,4,16,16]{4,3,2,1,0:T(8,128)(2,1)S(1)} %get-tuple-element.37, bf16[4,4,4,16,16]{4,3,2,1,0:T(8,128)(2,1)S(1)} %get-tuple-element.36, bf16[4,4,4,16,16]{4,3,2,1,0:T(8,128)(2,1)S(1)} %get-tuple-element.35, bf16[4,4,4,16,16]{4,3,2,1,0:T(8,128)(2,1)S(1)} %get-tuple-element.34, ...), dimensions={4} | concatenate | bytes 524288 | tf_op jit(solution)/shard_map/concatenate | solution.py:54
  34.5 0.8 fusion.1
  35.4 1.0 reshape.103
  36.4 2.0 %fusion.44 = (bf16[2,8,1,4,16,4,32]{6,5,4,3,2,1,0:T(4,128)(2,1)S(1)}, bf16[2,8,1,4,16,4,32]{6,5,4,3,2,1,0:T(4,128)(2,1)S(1)}, bf16[2,8,1,4,16,4,32]{6,5,4,3,2,1,...) fusion(bf16[2,9,2,4,16,4,32]{6,5,4,3,2,1,0:T(4,128)(2,1)S(1)} %reshape.103), kind=kLoop, calls=%fused_computation.92 | loop fusion | bytes 2097152 | tf_op jit(solution)/shard_map/slice | solution.py:67
  38.4 1.4 copy_bitcast_fusion.2
  39.8 1.4 copy_bitcast_fusion
  41.2 1.2 maximum_bitcast_fusion
  42.3 1.5 slice.167
  43.9 3.9 %compare_convert_fusion = (bf16[1,4,4,4,16,8,32]{6,5,4,3,2,1,0:T(8,128)(2,1)}, bf16[1,4,4,4,16,8,32]{6,5,4,3,2,1,0:T(8,128)(2,1)}, bf16[1,4,4,4,16,8,32]{6,5,4,3...) fusion(bf16[2,4,4,4,16,8,32]{6,5,4,3,2,1,0:T(8,128)(2,1)S(1)} %maximum_bitcast_fusion), kind=kLoop, calls=%fused_computation.5 | loop fusion | flops 2097152 | bytes 2621440 | tf_op jit(solution)/shard_map/convert_element_type | solution.py:70
  47.7 3.5 %squeeze.39 = bf16[64,4096]{1,0:T(8,128)(2,1)S(1)} reshape(bf16[1,4,4,4,16,8,32]{6,5,4,3,2,1,0:T(8,128)(2,1)} %slice.167) | data formatting | bytes 1048576 | tf_op jit(solution)/shard_map/squeeze | solution.py:71
  51.2 3.5 %reshape.114 = bf16[64,4096]{1,0:T(8,128)(2,1)S(1)} reshape(bf16[1,4,4,4,16,8,32]{6,5,4,3,2,1,0:T(8,128)(2,1)} %get-tuple-element.16) | data formatting | bytes 1048576 | tf_op jit(solution)/shard_map/convert_element_type | solution.py:70
  54.7 4.2 %reshape.112 = bf16[64,4096]{1,0:T(8,128)(2,1)} reshape(bf16[1,4,4,4,16,8,32]{6,5,4,3,2,1,0:T(8,128)(2,1)} %get-tuple-element.17) | data formatting | bytes 1048576 | tf_op jit(solution)/shard_map/convert_element_type | solution.py:70
  59.0 4.2 %reshape.113 = bf16[64,4096]{1,0:T(8,128)(2,1)} reshape(bf16[1,4,4,4,16,8,32]{6,5,4,3,2,1,0:T(8,128)(2,1)} %get-tuple-element.18) | data formatting | bytes 1048576 | tf_op jit(solution)/shard_map/convert_element_type | solution.py:70
  63.2 3.0 %reshape.111 = bf16[64,4096]{1,0:T(8,128)(2,1)} reshape(bf16[1,4,4,4,16,8,32]{6,5,4,3,2,1,0:T(8,128)(2,1)S(1)} %get-tuple-element.19) | data formatting | bytes 1048576 | tf_op jit(solution)/shard_map/convert_element_type | solution.py:70
  66.1 1.1 constant_dynamic-update-slice_fusion.12
  67.3 1.1 constant_dynamic-update-slice_fusion.11
  68.6 4.8 %convolution_convert_fusion = bf16[1024,4096]{1,0:T(8,128)(2,1)S(1)} fusion(bf16[320,1024]{1,0:T(8,128)(2,1)S(1)} %copy-done.5, bf16[320,4096]{1,0:T(8,128)(2,1)S(1)} %constant_dynamic-update-slice_fusion.8), kind=kOutput, calls=%fused_computation | convolution fusion | flops 2688548864 | bytes 11665408 | tf_op jit(solution)/shard_map/fm,fn->mn/dot_general | solution.py:37
  73.4 3.6 %multiply_convert_fusion = (bf16[128,4096]{1,0:T(8,128)(2,1)S(1)}, f32[128,4096]{1,0:T(8,128)}) fusion(bf16[1024,128]{1,0:T(8,128)(2,1)S(1)} %bitcast.117, bf16[1024,4096]{1,0:T(8,128)(2,1)S(1)} %convolution_convert_fusion), kind=kOutput, calls=%fused_computation.9 | convolution fusion | flops 1076363264 | bytes 11796480 | tf_op jit(solution)/shard_map/km,kn->mn/dot_general | solution.py:37
  77.9 23.0 %all_to_all.33 = bf16[64,16,256]{2,1,0:T(8,128)(2,1)S(1)} all-to-all(bf16[64,16,256]{2,1,0:T(8,128)(2,1)S(1)} %bitcast.110), channel_id=1, replica_groups=mesh['sy'=4,'sz'=8] {'sz'}, dimensions={0} | all-to-all | bytes 1048576 | tf_op jit(solution)/shard_map/all_to_all | solution.py:85
  101.0 1.5 fusion.3
  102.8 1.2 copy.53
  104.0 3.5 %all-to-all-start.1 = ((bf16[8,128,256]{2,0,1:T(8,128)(2,1)}), bf16[8,128,256]{2,0,1:T(8,128)(2,1)S(1)}, u32[]{:S(2)}, u32[]{:S(2)}) async-start(bf16[8,128,256]{2,0,1:T(8,128)(2,1)} %copy.53), calls=%async_computation.2 | async-start | bytes 1048576 | tf_op jit(solution)/shard_map/all_to_all | solution.py:91
  107.5 1.1 fusion.46
  108.7 14.1 %all-to-all-done.1 = bf16[8,128,256]{2,0,1:T(8,128)(2,1)S(1)} async-done(((bf16[8,128,256]{2,0,1:T(8,128)(2,1)}), bf16[8,128,256]{2,0,1:T(8,128)(2,1)S(1)}, u32[]{:S(2)}, u32[]{:S(2)}) %all-to-all-start.1) | async-done | bytes 524320 | tf_op jit(solution)/shard_map/all_to_all | solution.py:91
  122.7 6.6 %fusion.4 = f32[1024,128]{1,0:T(8,128)S(1)} fusion(bf16[1024,4096]{1,0:T(8,128)(2,1)} %copy-done.9, bf16[64,128]{0,1:T(8,128)(2,1)S(1)} %constant_dynamic-update-slice_fusion, bf16[64,4096]{1,0:T(8,128)(2,1)S(1)} %bitcast.105, f32[128,4096]{1,0:T(8,128)} %get-tuple-element.43), kind=kOutput, calls=%fused_computation.24 | convolution fusion | flops 1145569280 | bytes 11550720 | tf_op jit(solution)/shard_map/kn,mn->km/dot_general | solution.py:37
  130.0 0.5 fusion.47
  130.5 37.5 %psum.7 = f32[118,128]{1,0:T(8,128)S(1)} all-reduce(f32[118,128]{1,0:T(8,128)S(1)} %pad_maximum_fusion.1), channel_id=1, replica_groups=mesh['sy'=4,'sz'=8] {'sy','sz'}, use_global_device_ids=true, to_apply=%region_1.2 | all-reduce | flops 15104 | bytes 120832 | tf_op jit(solution)/shard_map/psum | solution.py:108
  168.0 0.7 copy.56
  168.9 0.8 copy.57
  169.7 1.6 broadcast_multiply_fusion
  (57 shorter events, 3.4 us)
Async XLA Ops:
  7.2 93.8 %copy-start = (bf16[8,128,128]{2,1,0:T(8,128)(2,1)S(1)}, bf16[8,128,128]{2,1,0:T(8,128)(2,1)}, u32[]{:S(2)}) copy-start(bf16[8,128,128]{2,1,0:T(8,128)(2,1)} %param.16) | copy-start | bytes 786436
  7.2 20.2 %copy-start.2 = (bf16[16,64,32]{1,2,0:T(8,128)(2,1)S(1)}, bf16[16,64,32]{1,2,0:T(8,128)(2,1)}, u32[]{:S(2)}) copy-start(bf16[16,64,32]{1,2,0:T(8,128)(2,1)} %param.11) | copy-start | bytes 196612
  9.4 15.0 %collective-permute-start = (bf16[2,16,1,32]{2,3,1,0:T(8,128)(2,1)S(1)}, bf16[2,16,1,32]{2,3,1,0:T(8,128)(2,1)S(1)}, u32[]{:S(2)}, u32[]{:S(2)}) collective-permute-start(bf16[2,16,1,32]{2,3,1,0:T(8,128)(2,1)S(1)} %get-tuple-element.28), channel_id=1, source_target_pairs={{0,8},{8,16},{16,24},{1,9},{9,17},{17,25},{2,10},{10,18},{18,26},{... | collective-permute-start | bytes 6152 | tf_op jit(solution)/shard_map/ppermute | solution.py:17
  14.2 13.1 %collective-permute-start.1 = (bf16[2,16,1,32]{2,3,1,0:T(8,128)(2,1)S(1)}, bf16[2,16,1,32]{2,3,1,0:T(8,128)(2,1)S(1)}, u32[]{:S(2)}, u32[]{:S(2)}) collective-permute-start(bf16[2,16,1,32]{2,3,1,0:T(8,128)(2,1)S(1)} %get-tuple-element.29), channel_id=1, source_target_pairs={{8,0},{16,8},{24,16},{9,1},{17,9},{25,17},{10,2},{18,10},{26,18},{... | collective-permute-start | bytes 6152 | tf_op jit(solution)/shard_map/ppermute | solution.py:18
  22.6 7.6 %copy-start.4 = (bf16[320,1024]{1,0:T(8,128)(2,1)}, bf16[320,1024]{1,0:T(8,128)(2,1)S(1)}, u32[]{:S(2)}) copy-start(bf16[320,1024]{1,0:T(8,128)(2,1)S(1)} %fusion.36) | copy-start | bytes 1966084
  27.5 7.0 %copy-start.7 = (bf16[66,128,1,1]{1,0,3,2:T(8,128)(2,1)S(1)}, bf16[66,128,1,1]{1,0,3,2:T(8,128)(2,1)}, u32[]{:S(2)}) copy-start(bf16[66,128,1,1]{1,0,3,2:T(8,128)(2,1)} %constant.71) | copy-start | bytes 50692
  27.5 7.0 %copy-start.8 = (bf16[34,64,1,1]{1,0,3,2:T(8,128)(2,1)S(1)}, bf16[34,64,1,1]{1,0,3,2:T(8,128)(2,1)}, u32[]{:S(2)}) copy-start(bf16[34,64,1,1]{1,0,3,2:T(8,128)(2,1)} %constant.72) | copy-start | bytes 13060
  27.5 7.0 %collective-permute-start.2 = (bf16[2,16,66,1]{2,3,1,0:T(2,128)(2,1)S(1)}, bf16[2,16,66,1]{2,3,1,0:T(2,128)(2,1)S(1)}, u32[]{:S(2)}, u32[]{:S(2)}) collective-permute-start(bf16[2,16,66,1]{2,3,1,0:T(2,128)(2,1)S(1)} %get-tuple-element.26), channel_id=1, source_target_pairs={{0,1},{1,2},{2,3},{3,4},{4,5},{5,6},{6,7},{8,9},{9,10},{10,11},{11... | collective-permute-start | bytes 12680 | tf_op jit(solution)/shard_map/ppermute | solution.py:17
  28.8 5.7 %collective-permute-start.3 = (bf16[2,16,66,1]{2,3,1,0:T(2,128)(2,1)S(1)}, bf16[2,16,66,1]{2,3,1,0:T(2,128)(2,1)S(1)}, u32[]{:S(2)}, u32[]{:S(2)}) collective-permute-start(bf16[2,16,66,1]{2,3,1,0:T(2,128)(2,1)S(1)} %get-tuple-element.27), channel_id=1, source_target_pairs={{1,0},{2,1},{3,2},{4,3},{5,4},{6,5},{7,6},{9,8},{10,9},{11,10},{12... | collective-permute-start | bytes 12680 | tf_op jit(solution)/shard_map/ppermute | solution.py:18
  66.1 2.3 %copy-start.1 = (bf16[64,4096]{1,0:T(8,128)(2,1)S(1)}, bf16[64,4096]{1,0:T(8,128)(2,1)}, u32[]{:S(2)}) copy-start(bf16[64,4096]{1,0:T(8,128)(2,1)} %reshape.113) | copy-start | bytes 1572868
  67.3 1.3 copy-start.5
  68.6 4.8 %copy-start.3 = (bf16[4,4,4,16,128]{4,3,2,1,0:T(8,128)(2,1)S(1)}, bf16[4,4,4,16,128]{4,3,2,1,0:T(8,128)(2,1)}, u32[]{:S(2)}) copy-start(bf16[4,4,4,16,128]{4,3,2,1,0:T(8,128)(2,1)} %concatenate.23) | copy-start | bytes 786436
  73.4 4.0 %copy-start.9 = (bf16[1024,4096]{1,0:T(8,128)(2,1)}, bf16[1024,4096]{1,0:T(8,128)(2,1)S(1)}, u32[]{:S(2)}) copy-start(bf16[1024,4096]{1,0:T(8,128)(2,1)S(1)} %convolution_convert_fusion) | copy-start | bytes 25165828
  77.4 23.5 %copy-start.6 = (bf16[8,8,32,128]{3,2,1,0:T(8,128)(2,1)S(1)}, bf16[8,8,32,128]{3,2,1,0:T(8,128)(2,1)}, u32[]{:S(2)}) copy-start(bf16[8,8,32,128]{3,2,1,0:T(8,128)(2,1)} %param.17) | copy-start | bytes 1572868
  104.0 18.8 %all-to-all-start.1 = ((bf16[8,128,256]{2,0,1:T(8,128)(2,1)}), bf16[8,128,256]{2,0,1:T(8,128)(2,1)S(1)}, u32[]{:S(2)}, u32[]{:S(2)}) async-start(bf16[8,128,256]{2,0,1:T(8,128)(2,1)} %copy.53), calls=%async_computation.2 | async-start | bytes 1048576 | tf_op jit(solution)/shard_map/all_to_all | solution.py:91
  107.5 62.3 %reduce-scatter.2.cloned.1.call-start = ((), (), s32[]{:S(2)}) async-start(), calls=%async_computation.3 | async-start | bytes 655360 | tf_op jit(solution)/shard_map/reduce_scatter | solution.py:94
Sparse Core Ops, SparseCore 0:
  111.1 25.3 reduce-scatter.1
where the time goes:
time: 180 us; the launch traced here: 178 us
  blocking collectives  60.6 us (34%)
  local copies, waits for them, and re-layouts  44.7 us (25%)
  matrix products  19.6 us (11%)
  waiting for transfers between devices  17.1 us (10%)
  between operations  14.5 us (8%)
  starting transfers between devices  12.3 us (7%)
  other arithmetic  9.53 us (5%)
    psum x1, blocking collectives, per_device(): parts = lax.psum(parts, ('sy', 'sz'))  37.5 us
    all_to_all x1, blocking collectives, per_device(): lax.all_to_all(coarse, 'sz', split_axis=0, concat_axis=1, tiled=True)  23 us
    dot_general x9, matrix products, dot(): return jnp.einsum(spec, left, right, preferred_element_type=jnp.float32)  19.6 us
    convert_element_type x4, local copies, waits for them, and re-layouts, per_device(): (windows[0] == entry + 1).astype(jnp.bfloat16)  14.9 us
    all_to_all x1, waiting for transfers between devices, per_device(): lax.all_to_all(channel_grad, 'sz', split_axis=1, concat_axis=0, tiled=True)  14.1 us
    unnamed x34, local copies, waits for them, and re-layouts  9.62 us
    ppermute x2, starting transfers between devices, extended(): before = lax.ppermute(last, axis, up)  6.15 us
    concatenate x1, local copies, waits for them, and re-layouts, per_device(): jnp.concatenate([jnp.pad(taps, ((a, 1 - a), (b, 1 - b), (c, 1 - c), (0, 0...  3.91 us
  transfers between devices with their start and end apart: 6, of which 2 were waited for; matrix products, arithmetic and copies ran while one was open for 13% of the time, Pallas kernels for 0%

commit v1 on v0

--- a/solution.py
+++ b/solution.py
@@ -1,9 +1,12 @@
+import functools
 import math
 
 import jax
 import jax.numpy as jnp
 import numpy as np
 from jax import lax
+from jax.experimental import pallas as pl
+from jax.experimental.pallas import tpu as pltpu
 from jax.sharding import PartitionSpec as P
 
 
@@ -35,6 +38,83 @@
 
 def dot(spec, left, right):
     return jnp.einsum(spec, left, right, preferred_element_type=jnp.float32)
+
+
+def total_kernel(count_y, count_z, x_ref, out_ref, first, second, gathered, s1, r1, s2, r2, s3, r3):
+    my_y, my_z = lax.axis_index("sy"), lax.axis_index("sz")
+    peers_y = [{"sy": lax.rem(my_y + d, count_y)} for d in range(1, count_y)]
+    peers_z = [{"sz": lax.rem(my_z + d, count_z)} for d in range(1, count_z)]
+
+    def send(src, dst, send_sem, recv_sem, peer):
+        copy = pltpu.make_async_remote_copy(
+            src_ref=src,
+            dst_ref=dst,
+            send_sem=send_sem,
+            recv_sem=recv_sem,
+            device_id=peer,
+            device_id_type=pl.DeviceIdType.MESH,
+        )
+        copy.start()
+        return copy
+
+    barrier = pltpu.get_barrier_semaphore()
+    for peer in peers_y + peers_z:
+        pl.semaphore_signal(barrier, inc=1, device_id=peer, device_id_type=pl.DeviceIdType.MESH)
+    pl.semaphore_wait(barrier, count_y + count_z - 2)
+
+    copies = [
+        send(x_ref.at[peer["sz"]], first.at[d], s1.at[d], r1.at[d], peer)
+        for d, peer in enumerate(peers_z)
+    ]
+    total = x_ref[my_z]
+    for d, copy in enumerate(copies):
+        copy.wait()
+        total = total + first[d]
+    second[my_y] = total
+    copies = [
+        send(second.at[my_y], second.at[my_y], s2.at[d], r2.at[d], peer)
+        for d, peer in enumerate(peers_y)
+    ]
+    for copy in copies:
+        copy.wait()
+    total = second[0]
+    for entry in range(1, count_y):
+        total = total + second[entry]
+    gathered[my_z] = total
+    copies = [
+        send(gathered.at[my_z], gathered.at[my_z], s3.at[d], r3.at[d], peer)
+        for d, peer in enumerate(peers_z)
+    ]
+    for copy in copies:
+        copy.wait()
+    out_ref[...] = gathered[...]
+
+
+def total_of(parts, count_y, count_z):
+    rows, lanes = parts.shape
+    chunk = -(-rows // (8 * count_z)) * 8
+    padded = jnp.pad(parts, ((0, chunk * count_z - rows), (0, 0)))
+    whole = (count_z, chunk, lanes)
+    dma = pltpu.SemaphoreType.DMA
+    summed = pl.pallas_call(
+        functools.partial(total_kernel, count_y, count_z),
+        out_shape=jax.ShapeDtypeStruct(whole, jnp.float32),
+        in_specs=[pl.BlockSpec(memory_space=pltpu.VMEM)],
+        out_specs=pl.BlockSpec(memory_space=pltpu.VMEM),
+        scratch_shapes=[
+            pltpu.VMEM((count_z - 1, chunk, lanes), jnp.float32),
+            pltpu.VMEM((count_y, chunk, lanes), jnp.float32),
+            pltpu.VMEM(whole, jnp.float32),
+            dma((count_z - 1,)),
+            dma((count_z - 1,)),
+            dma((count_y - 1,)),
+            dma((count_y - 1,)),
+            dma((count_z - 1,)),
+            dma((count_z - 1,)),
+        ],
+        compiler_params=pltpu.CompilerParams(collective_id=0, has_side_effects=True),
+    )(padded.reshape(whole))
+    return summed.reshape(chunk * count_z, lanes)[:rows]
 
 
 def per_device(
@@ -105,7 +185,7 @@
     )
     width = 8 * channels
     parts = jnp.concatenate([down_partial, conv_partial.reshape(-1, width)], axis=0)
-    parts = lax.psum(parts, ("sy", "sz"))
+    parts = total_of(parts, count_y, count_z)
     cells_fine = depth * rows_y * count_y * rows_z * count_z
     cells_coarse = cells_fine // 8
     down_total = parts[:wide_channels].reshape(wide_channels, 8, channels)

time: 180 us -> 158 us (0.88)
  blocking collectives: 60.6 us -> 23 us
  Pallas kernels: 0 us -> 13.9 us
  other arithmetic: 9.53 us -> 11.7 us
    psum x1 -> x0, blocking collectives: 37.5 us -> none  [per_device(): parts = lax.psum(parts, ('sy', 'sz'))]
    pallas_call x0 -> x1, Pallas kernels: none -> 13.9 us  [total_of(): pl.pallas_call(functools.partial(total_kernel, count_y, count_z), out_sha...]
    unnamed x34 -> x35, local copies, waits for them, and re-layouts: 9.62 us -> 10.4 us
  transfers between devices with their start and end apart: 6 -> 6, of which waited for: 2 -> 2; matrix products, arithmetic and copies ran while one was open for 13% -> 17% of each run, Pallas kernels for 0% -> 9%
where the time goes in v1:
time: 158 us; the launch traced here: 157 us
  local copies, waits for them, and re-layouts  44.8 us (28%)
  blocking collectives  23 us (15%)
  matrix products  19.6 us (12%)
  waiting for transfers between devices  16.8 us (11%)
  between operations  14.5 us (9%)
  Pallas kernels  13.9 us (9%)
  starting transfers between devices  12.5 us (8%)
  other arithmetic  11.7 us (7%)
    all_to_all x1, blocking collectives, per_device(): lax.all_to_all(coarse, 'sz', split_axis=0, concat_axis=1, tiled=True)  23 us
    dot_general x9, matrix products, dot(): return jnp.einsum(spec, left, right, preferred_element_type=jnp.float32)  19.6 us
    convert_element_type x4, local copies, waits for them, and re-layouts, per_device(): (windows[0] == entry + 1).astype(jnp.bfloat16)  14.9 us
    pallas_call x1, Pallas kernels, total_of(): pl.pallas_call(functools.partial(total_kernel, count_y, count_z), out_sha...  13.9 us
    all_to_all x1, waiting for transfers between devices, per_device(): lax.all_to_all(channel_grad, 'sz', split_axis=1, concat_axis=0, tiled=True)  13.8 us
    unnamed x35, local copies, waits for them, and re-layouts  10.4 us
    ppermute x2, starting transfers between devices, extended(): before = lax.ppermute(last, axis, up)  6.15 us
    concatenate x1, local copies, waits for them, and re-layouts, per_device(): jnp.concatenate([jnp.pad(taps, ((a, 1 - a), (b, 1 - b), (c, 1 - c), (0, 0...  3.91 us
  transfers between devices with their start and end apart: 6, of which 2 were waited for; matrix products, arithmetic and copies ran while one was open for 17% of the time, Pallas kernels for 9%

profile of v1, /device:TPU:0, one launch (start us, length us, event | category | flops | bytes accessed | tf_op | source)
XLA Modules:
  0.0 156.8 jit_solution(8842273308458864750)
XLA Ops:
  7.2 1.0 fusion.37
  8.2 1.1 slice_maximum_fusion
  9.4 4.9 %collective-permute-start = (bf16[2,16,1,32]{2,3,1,0:T(8,128)(2,1)S(1)}, bf16[2,16,1,32]{2,3,1,0:T(8,128)(2,1)S(1)}, u32[]{:S(2)}, u32[]{:S(2)}) collective-permute-start(bf16[2,16,1,32]{2,3,1,0:T(8,128)(2,1)S(1)} %get-tuple-element.28), channel_id=1, source_target_pairs={{0,8},{8,16},{16,24},{1,9},{9,17},{17,25},{2,10},{10,18},{18,26},{... | collective-permute-start | bytes 6152 | tf_op jit(solution)/shard_map/ppermute | solution.py:20
  14.2 1.3 collective-permute-start.1
  15.6 0.8 slice_bitcast_fusion
  17.5 0.7 constant_dynamic-update-slice_fusion.7
  18.2 0.7 constant_dynamic-update-slice_fusion.6
  18.9 0.7 constant_dynamic-update-slice_fusion.5
  19.6 0.7 constant_dynamic-update-slice_fusion.4
  20.3 0.7 constant_dynamic-update-slice_fusion.3
  21.0 0.7 constant_dynamic-update-slice_fusion.2
  21.7 0.7 constant_dynamic-update-slice_fusion.1
  22.6 0.7 constant_dynamic-update-slice_fusion
  23.3 1.0 copy.44
  24.3 3.0 %collective-permute-done.1 = bf16[2,16,1,32]{2,3,1,0:T(8,128)(2,1)S(1)} collective-permute-done((bf16[2,16,1,32]{2,3,1,0:T(8,128)(2,1)S(1)}, bf16[2,16,1,32]{2,3,1,0:T(8,128)(2,1)S(1)}, u32[]{:S(2)}, u32[]{:S(2)}) %collective-permute-start.1) | collective-permute-done | bytes 2080 | tf_op jit(solution)/shard_map/ppermute | solution.py:21
  27.5 1.3 collective-permute-start.2
  28.8 1.3 collective-permute-start.3
  30.6 3.9 %concatenate.23 = bf16[4,4,4,16,128]{4,3,2,1,0:T(8,128)(2,1)} concatenate(bf16[4,4,4,16,16]{4,3,2,1,0:T(8,128)(2,1)S(1)} %get-tuple-element.37, bf16[4,4,4,16,16]{4,3,2,1,0:T(8,128)(2,1)S(1)} %get-tuple-element.36, bf16[4,4,4,16,16]{4,3,2,1,0:T(8,128)(2,1)S(1)} %get-tuple-element.35, bf16[4,4,4,16,16]{4,3,2,1,0:T(8,128)(2,1)S(1)} %get-tuple-element.34, ...), dimensions={4} | concatenate | bytes 524288 | tf_op jit(solution)/shard_map/concatenate | solution.py:134
  34.5 0.8 fusion.1
  35.4 1.0 reshape.111
  36.4 2.0 %fusion.44 = (bf16[2,8,1,4,16,4,32]{6,5,4,3,2,1,0:T(4,128)(2,1)S(1)}, bf16[2,8,1,4,16,4,32]{6,5,4,3,2,1,0:T(4,128)(2,1)S(1)}, bf16[2,8,1,4,16,4,32]{6,5,4,3,2,1,...) fusion(bf16[2,9,2,4,16,4,32]{6,5,4,3,2,1,0:T(4,128)(2,1)S(1)} %reshape.111), kind=kLoop, calls=%fused_computation.93 | loop fusion | bytes 2097152 | tf_op jit(solution)/shard_map/slice | solution.py:147
  38.5 1.4 copy_bitcast_fusion.2
  39.8 1.4 copy_bitcast_fusion
  41.2 1.2 maximum_bitcast_fusion
  42.3 1.5 slice.171
  43.9 3.9 %compare_convert_fusion = (bf16[1,4,4,4,16,8,32]{6,5,4,3,2,1,0:T(8,128)(2,1)}, bf16[1,4,4,4,16,8,32]{6,5,4,3,2,1,0:T(8,128)(2,1)}, bf16[1,4,4,4,16,8,32]{6,5,4,3...) fusion(bf16[2,4,4,4,16,8,32]{6,5,4,3,2,1,0:T(8,128)(2,1)S(1)} %maximum_bitcast_fusion), kind=kLoop, calls=%fused_computation.5 | loop fusion | flops 2097152 | bytes 2621440 | tf_op jit(solution)/shard_map/convert_element_type | solution.py:150
  47.7 3.5 %squeeze.39 = bf16[64,4096]{1,0:T(8,128)(2,1)S(1)} reshape(bf16[1,4,4,4,16,8,32]{6,5,4,3,2,1,0:T(8,128)(2,1)} %slice.171) | data formatting | bytes 1048576 | tf_op jit(solution)/shard_map/squeeze | solution.py:151
  51.2 3.5 %reshape.124 = bf16[64,4096]{1,0:T(8,128)(2,1)S(1)} reshape(bf16[1,4,4,4,16,8,32]{6,5,4,3,2,1,0:T(8,128)(2,1)} %get-tuple-element.16) | data formatting | bytes 1048576 | tf_op jit(solution)/shard_map/convert_element_type | solution.py:150
  54.8 4.2 %reshape.122 = bf16[64,4096]{1,0:T(8,128)(2,1)} reshape(bf16[1,4,4,4,16,8,32]{6,5,4,3,2,1,0:T(8,128)(2,1)} %get-tuple-element.17) | data formatting | bytes 1048576 | tf_op jit(solution)/shard_map/convert_element_type | solution.py:150
  59.0 4.2 %reshape.123 = bf16[64,4096]{1,0:T(8,128)(2,1)} reshape(bf16[1,4,4,4,16,8,32]{6,5,4,3,2,1,0:T(8,128)(2,1)} %get-tuple-element.18) | data formatting | bytes 1048576 | tf_op jit(solution)/shard_map/convert_element_type | solution.py:150
  63.2 3.0 %reshape.121 = bf16[64,4096]{1,0:T(8,128)(2,1)} reshape(bf16[1,4,4,4,16,8,32]{6,5,4,3,2,1,0:T(8,128)(2,1)S(1)} %get-tuple-element.19) | data formatting | bytes 1048576 | tf_op jit(solution)/shard_map/convert_element_type | solution.py:150
  66.2 1.1 constant_dynamic-update-slice_fusion.12
  67.3 1.1 constant_dynamic-update-slice_fusion.11
  68.6 4.8 %convolution_convert_fusion = bf16[1024,4096]{1,0:T(8,128)(2,1)S(1)} fusion(bf16[320,1024]{1,0:T(8,128)(2,1)S(1)} %copy-done.5, bf16[320,4096]{1,0:T(8,128)(2,1)S(1)} %constant_dynamic-update-slice_fusion.8), kind=kOutput, calls=%fused_computation | convolution fusion | flops 2688548864 | bytes 11665408 | tf_op jit(solution)/shard_map/fm,fn->mn/dot_general | solution.py:40
  73.4 3.6 %multiply_convert_fusion = (bf16[128,4096]{1,0:T(8,128)(2,1)S(1)}, f32[128,4096]{1,0:T(8,128)}) fusion(bf16[1024,128]{1,0:T(8,128)(2,1)S(1)} %bitcast.118, bf16[1024,4096]{1,0:T(8,128)(2,1)S(1)} %convolution_convert_fusion), kind=kOutput, calls=%fused_computation.9 | convolution fusion | flops 1076363264 | bytes 11796480 | tf_op jit(solution)/shard_map/km,kn->mn/dot_general | solution.py:40
  77.9 23.0 %all_to_all.33 = bf16[64,16,256]{2,1,0:T(8,128)(2,1)S(1)} all-to-all(bf16[64,16,256]{2,1,0:T(8,128)(2,1)S(1)} %bitcast.110), channel_id=1, replica_groups=mesh['sy'=4,'sz'=8] {'sz'}, dimensions={0} | all-to-all | bytes 1048576 | tf_op jit(solution)/shard_map/all_to_all | solution.py:165
  101.0 1.5 fusion.3
  102.8 1.2 copy.52
  104.0 3.5 %all-to-all-start.1 = ((bf16[8,128,256]{2,0,1:T(8,128)(2,1)}), bf16[8,128,256]{2,0,1:T(8,128)(2,1)S(1)}, u32[]{:S(2)}, u32[]{:S(2)}) async-start(bf16[8,128,256]{2,0,1:T(8,128)(2,1)} %copy.52), calls=%async_computation.2 | async-start | bytes 1048576 | tf_op jit(solution)/shard_map/all_to_all | solution.py:171
  107.7 1.2 fusion.46
  108.9 13.8 %all-to-all-done.1 = bf16[8,128,256]{2,0,1:T(8,128)(2,1)S(1)} async-done(((bf16[8,128,256]{2,0,1:T(8,128)(2,1)}), bf16[8,128,256]{2,0,1:T(8,128)(2,1)S(1)}, u32[]{:S(2)}, u32[]{:S(2)}) %all-to-all-start.1) | async-done | bytes 524320 | tf_op jit(solution)/shard_map/all_to_all | solution.py:171
  122.8 6.6 %fusion.4 = f32[1024,128]{1,0:T(8,128)S(1)} fusion(bf16[1024,4096]{1,0:T(8,128)(2,1)} %copy-done.9, bf16[64,128]{0,1:T(8,128)(2,1)S(1)} %constant_dynamic-update-slice_fusion, bf16[64,4096]{1,0:T(8,128)(2,1)S(1)} %bitcast.105, f32[128,4096]{1,0:T(8,128)} %get-tuple-element.43), kind=kOutput, calls=%fused_computation.24 | convolution fusion | flops 1145569280 | bytes 11550720 | tf_op jit(solution)/shard_map/kn,mn->km/dot_general | solution.py:40
  131.1 13.9 %shard_map.129 = f32[8,16,128]{2,1,0:T(8,128)} custom-call(f32[8,16,128]{2,1,0:T(8,128)} %bitcast.119), custom_call_target="tpu_custom_call" | custom-call | tf_op jit(solution)/shard_map/pallas_call | solution.py:99
  145.0 0.8 slice_multiply_fusion.1
  145.9 0.8 copy.56
  146.7 0.8 slice_multiply_fusion
  147.6 0.8 copy.55
  148.4 1.6 %broadcast_multiply_fusion = f32[8,32,128]{2,1,0:T(8,128)} fusion(f32[8,32,128]{2,1,0:T(8,128)} %reduce-scatter.2.cloned.1.call-done), kind=kLoop, calls=%fused_computation.60 | loop fusion | flops 32768 | bytes 262144 | tf_op jit(solution)/shard_map/div | solution.py:174
  (58 shorter events, 5.5 us)
Async XLA Ops:
  7.2 93.8 %copy-start = (bf16[8,128,128]{2,1,0:T(8,128)(2,1)S(1)}, bf16[8,128,128]{2,1,0:T(8,128)(2,1)}, u32[]{:S(2)}) copy-start(bf16[8,128,128]{2,1,0:T(8,128)(2,1)} %param.16) | copy-start | bytes 786436
  7.2 20.2 %copy-start.2 = (bf16[16,64,32]{1,2,0:T(8,128)(2,1)S(1)}, bf16[16,64,32]{1,2,0:T(8,128)(2,1)}, u32[]{:S(2)}) copy-start(bf16[16,64,32]{1,2,0:T(8,128)(2,1)} %param.11) | copy-start | bytes 196612
  9.4 15.0 %collective-permute-start = (bf16[2,16,1,32]{2,3,1,0:T(8,128)(2,1)S(1)}, bf16[2,16,1,32]{2,3,1,0:T(8,128)(2,1)S(1)}, u32[]{:S(2)}, u32[]{:S(2)}) collective-permute-start(bf16[2,16,1,32]{2,3,1,0:T(8,128)(2,1)S(1)} %get-tuple-element.28), channel_id=1, source_target_pairs={{0,8},{8,16},{16,24},{1,9},{9,17},{17,25},{2,10},{10,18},{18,26},{... | collective-permute-start | bytes 6152 | tf_op jit(solution)/shard_map/ppermute | solution.py:20
  14.2 13.1 %collective-permute-start.1 = (bf16[2,16,1,32]{2,3,1,0:T(8,128)(2,1)S(1)}, bf16[2,16,1,32]{2,3,1,0:T(8,128)(2,1)S(1)}, u32[]{:S(2)}, u32[]{:S(2)}) collective-permute-start(bf16[2,16,1,32]{2,3,1,0:T(8,128)(2,1)S(1)} %get-tuple-element.29), channel_id=1, source_target_pairs={{8,0},{16,8},{24,16},{9,1},{17,9},{25,17},{10,2},{18,10},{26,18},{... | collective-permute-start | bytes 6152 | tf_op jit(solution)/shard_map/ppermute | solution.py:21
  22.6 7.6 %copy-start.4 = (bf16[320,1024]{1,0:T(8,128)(2,1)}, bf16[320,1024]{1,0:T(8,128)(2,1)S(1)}, u32[]{:S(2)}) copy-start(bf16[320,1024]{1,0:T(8,128)(2,1)S(1)} %fusion.36) | copy-start | bytes 1966084
  27.5 7.0 %copy-start.7 = (bf16[66,128,1,1]{1,0,3,2:T(8,128)(2,1)S(1)}, bf16[66,128,1,1]{1,0,3,2:T(8,128)(2,1)}, u32[]{:S(2)}) copy-start(bf16[66,128,1,1]{1,0,3,2:T(8,128)(2,1)} %constant.75) | copy-start | bytes 50692
  27.5 7.0 %copy-start.8 = (bf16[34,64,1,1]{1,0,3,2:T(8,128)(2,1)S(1)}, bf16[34,64,1,1]{1,0,3,2:T(8,128)(2,1)}, u32[]{:S(2)}) copy-start(bf16[34,64,1,1]{1,0,3,2:T(8,128)(2,1)} %constant.76) | copy-start | bytes 13060
  27.5 7.0 %collective-permute-start.2 = (bf16[2,16,66,1]{2,3,1,0:T(2,128)(2,1)S(1)}, bf16[2,16,66,1]{2,3,1,0:T(2,128)(2,1)S(1)}, u32[]{:S(2)}, u32[]{:S(2)}) collective-permute-start(bf16[2,16,66,1]{2,3,1,0:T(2,128)(2,1)S(1)} %get-tuple-element.26), channel_id=1, source_target_pairs={{0,1},{1,2},{2,3},{3,4},{4,5},{5,6},{6,7},{8,9},{9,10},{10,11},{11... | collective-permute-start | bytes 12680 | tf_op jit(solution)/shard_map/ppermute | solution.py:20
  28.8 5.7 %collective-permute-start.3 = (bf16[2,16,66,1]{2,3,1,0:T(2,128)(2,1)S(1)}, bf16[2,16,66,1]{2,3,1,0:T(2,128)(2,1)S(1)}, u32[]{:S(2)}, u32[]{:S(2)}) collective-permute-start(bf16[2,16,66,1]{2,3,1,0:T(2,128)(2,1)S(1)} %get-tuple-element.27), channel_id=1, source_target_pairs={{1,0},{2,1},{3,2},{4,3},{5,4},{6,5},{7,6},{9,8},{10,9},{11,10},{12... | collective-permute-start | bytes 12680 | tf_op jit(solution)/shard_map/ppermute | solution.py:21
  66.2 2.3 %copy-start.1 = (bf16[64,4096]{1,0:T(8,128)(2,1)S(1)}, bf16[64,4096]{1,0:T(8,128)(2,1)}, u32[]{:S(2)}) copy-start(bf16[64,4096]{1,0:T(8,128)(2,1)} %reshape.123) | copy-start | bytes 1572868
  67.3 1.3 copy-start.5
  68.6 4.8 %copy-start.3 = (bf16[4,4,4,16,128]{4,3,2,1,0:T(8,128)(2,1)S(1)}, bf16[4,4,4,16,128]{4,3,2,1,0:T(8,128)(2,1)}, u32[]{:S(2)}) copy-start(bf16[4,4,4,16,128]{4,3,2,1,0:T(8,128)(2,1)} %concatenate.23) | copy-start | bytes 786436
  73.4 4.0 %copy-start.9 = (bf16[1024,4096]{1,0:T(8,128)(2,1)}, bf16[1024,4096]{1,0:T(8,128)(2,1)S(1)}, u32[]{:S(2)}) copy-start(bf16[1024,4096]{1,0:T(8,128)(2,1)S(1)} %convolution_convert_fusion) | copy-start | bytes 25165828
  77.4 23.5 %copy-start.6 = (bf16[8,8,32,128]{3,2,1,0:T(8,128)(2,1)S(1)}, bf16[8,8,32,128]{3,2,1,0:T(8,128)(2,1)}, u32[]{:S(2)}) copy-start(bf16[8,8,32,128]{3,2,1,0:T(8,128)(2,1)} %param.17) | copy-start | bytes 1572868
  104.0 18.8 %all-to-all-start.1 = ((bf16[8,128,256]{2,0,1:T(8,128)(2,1)}), bf16[8,128,256]{2,0,1:T(8,128)(2,1)S(1)}, u32[]{:S(2)}, u32[]{:S(2)}) async-start(bf16[8,128,256]{2,0,1:T(8,128)(2,1)} %copy.52), calls=%async_computation.2 | async-start | bytes 1048576 | tf_op jit(solution)/shard_map/all_to_all | solution.py:171
  107.5 40.9 %reduce-scatter.2.cloned.1.call-start = ((), (), s32[]{:S(2)}) async-start(), calls=%async_computation.3 | async-start | bytes 655360 | tf_op jit(solution)/shard_map/reduce_scatter | solution.py:174
Sparse Core Ops, SparseCore 0:
  111.1 25.2 reduce-scatter.1
